TPU v7x, 32 devices: a whole 2x2x4 slice. The times are simulated.
32 devices in a mesh: fsdp: 2 (over x), ctx: 4 (over z), tp: 4 (over y, core).
Axes of the slice: x: 2, y: 2, z: 4, core: 2. Of those that a mesh axis runs over, the one named last changes fastest.
Arguments:
- tokens: bfloat16 [3, 2, 1024, 768], P(None, 'fsdp', ('ctx', 'tp')), may hold values from -6 to 6
- positions: int32 [3, 2, 1024], P(None, 'fsdp', 'ctx'), may hold values from 0 to 1535, as said below
- w_query: bfloat16 [768, 768], P('fsdp', 'tp'), may hold values from -0.109375 to 0.109375
- w_key: bfloat16 [768, 768], P('fsdp', 'tp'), may hold values from -0.109375 to 0.109375
- w_value: bfloat16 [768, 768], P('fsdp', 'tp'), may hold values from -0.21875 to 0.21875
- w_out: bfloat16 [768, 768], P('tp', 'fsdp'), may hold values from -1.75 to 1.75
- w_in: bfloat16 [768, 3072], P('fsdp', 'tp'), may hold values from -0.21875 to 0.21875
- w_back: bfloat16 [3072, 768], P('tp', 'fsdp'), may hold values from -0.109375 to 0.109375
- gain_one: bfloat16 [768], P('fsdp'), may hold values from 0.5 to 1.5
- gain_two: bfloat16 [768], P('fsdp'), may hold values from 0.5 to 1.5
- bias_table: bfloat16 [32, 12], P('fsdp', 'tp'), may hold values from -4 to 4
- cotangent: bfloat16 [3, 2, 1024, 768], P(None, 'fsdp', ('ctx', 'tp')), may hold values from -6 to 6
Outputs:
- output: bfloat16 [3, 2, 1024, 768], P(None, 'fsdp', ('ctx', 'tp'))
- input_grad: bfloat16 [3, 2, 1024, 768], P(None, 'fsdp', ('ctx', 'tp'))
- gain_one_grad: float32 [768], P('fsdp')
- gain_two_grad: float32 [768], P('fsdp')
- query_grad: float32 [768, 768], P('fsdp', 'tp')
- key_grad: float32 [768, 768], P('fsdp', 'tp')
- value_grad: float32 [768, 768], P('fsdp', 'tp')
- out_grad: float32 [768, 768], P('tp', 'fsdp')
- in_grad: float32 [768, 3072], P('fsdp', 'tp')
- back_grad: float32 [3072, 768], P('tp', 'fsdp')
- table_grad: float32 [32, 12], P('fsdp', 'tp')
Inputs may be any that keep to these rules, and one draw needn't show every extreme that they name: Within each sequence the positions start at 0 and rise by 1 or 2 from one token to the next; exactly 512 of the steps rise by 2, so the last position is 1535.
All inputs are finite; a program needn't handle non-finite values.
Results may differ from a plain program's by a relative error of at most 0.02.
Values may be sent and summed in bfloat16 or wider, within the bound.
A program may use at most 128 MiB of HBM per device.

v0:
```python
import math

import jax
import jax.numpy as jnp
from jax import lax
from jax.sharding import PartitionSpec as P

D = 768
HDIM = 64


epsilon = 1e-06
bucket_edges = (12, 16, 23, 32, 46, 64, 91)


def bucket_of(query_pos, key_pos):
    relative = (key_pos[None, :] - query_pos[:, None]).astype(jnp.int32)
    magnitude = jnp.abs(relative)
    bucket = jnp.minimum(magnitude, 8)
    for edge_value in bucket_edges:
        bucket = bucket + (magnitude >= edge_value).astype(jnp.int32)
    return bucket + 16 * (relative > 0).astype(jnp.int32)


def table_bias(bucket, bias_rows):
    slot_ids = jnp.arange(bias_rows.shape[0], dtype=jnp.int32)
    matches = bucket[None, :, :, None] == slot_ids[None, None, None, :]
    return jnp.sum(jnp.where(matches, bias_rows.T[:, None, None, :], 0.0), axis=-1)


def table_grad(bucket, grad_scores, bucket_count):
    slot_ids = jnp.arange(bucket_count, dtype=jnp.int32)
    matches = bucket[None, None, :, :] == slot_ids[:, None, None, None]
    return jnp.sum(jnp.where(matches, grad_scores[None], 0.0), axis=(2, 3))


def inverse_rms(token_rows):
    return lax.rsqrt(jnp.mean(token_rows * token_rows, axis=-1, keepdims=True) + epsilon)


def norm_back(token_rows, scale_rows, gain_full, grad_normed):
    weighted = gain_full * grad_normed
    grad_rows = scale_rows * weighted - token_rows * scale_rows**3 * jnp.mean(
        token_rows * weighted, axis=-1, keepdims=True
    )
    return (grad_rows, jnp.sum(grad_normed * token_rows * scale_rows, axis=0))


def gelu_slope(values_in):
    return (
        0.5 * (1.0 + jax.scipy.special.erf(values_in * 0.7071067811865476))
        + values_in * jnp.exp(-0.5 * values_in * values_in) * 0.3989422804014327
    )


def left_product(left, right):
    return jnp.einsum("ra,rb->ab", left, right, preferred_element_type=jnp.float32)


def right_product(left, right):
    return jnp.einsum("ra,ba->rb", left, right, preferred_element_type=jnp.float32)


def spread_rows(local_rows):
    return lax.all_gather(local_rows, "tp", axis=0, tiled=True)


def collect_rows(partial_rows):
    return lax.psum_scatter(
        partial_rows.astype(jnp.bfloat16), "tp", scatter_dimension=0, tiled=True
    ).astype(jnp.float32)


def pair_terms(
    query_block,
    query_pos,
    key_block,
    key_pos,
    value_block,
    grad_att,
    log_total,
    row_delta,
    bias_rows,
):
    bucket = bucket_of(query_pos, key_pos)
    scores = jnp.einsum("qhd,khd->hqk", query_block, key_block, preferred_element_type=jnp.float32)
    scores = scores + table_bias(bucket, bias_rows)
    probability = jnp.exp(scores - log_total[:, :, None])
    grad_prob = jnp.einsum(
        "qhd,khd->hqk", grad_att, value_block, preferred_element_type=jnp.float32
    )
    grad_scores = probability * (grad_prob - row_delta[:, :, None])
    return (bucket, probability, grad_scores)


def make_fold(queries, query_pos, bias_rows, key_rows):
    head_count = queries.shape[1]

    def fold_keys(state_carry, shard_piece, first_row):
        keys_part, values_part, pos_part = shard_piece
        block_count = keys_part.shape[0] // key_rows
        key_blocks = keys_part.reshape(block_count, key_rows, head_count, HDIM)
        value_blocks = values_part.reshape(block_count, key_rows, head_count, HDIM)
        pos_blocks = pos_part.reshape(block_count, key_rows)

        def fold_one_block(inner, block_item):
            run_peak, run_total, run_acc = inner
            key_block, value_block, pos_block = block_item
            scores = jnp.einsum(
                "qhd,khd->hqk", queries, key_block, preferred_element_type=jnp.float32
            )
            scores = scores + table_bias(bucket_of(query_pos, pos_block), bias_rows)
            new_peak = jnp.maximum(run_peak, jnp.max(scores, axis=-1))
            factor = jnp.exp(run_peak - new_peak)
            weights_exp = jnp.exp(scores - new_peak[:, :, None])
            run_total = run_total * factor + jnp.sum(weights_exp, axis=-1)
            run_acc = run_acc * factor[:, :, None] + jnp.einsum(
                "hqk,khd->hqd",
                weights_exp.astype(jnp.bfloat16),
                value_block,
                preferred_element_type=jnp.float32,
            )
            return ((new_peak, run_total, run_acc), None)

        result, unused = lax.scan(
            fold_one_block, state_carry, (key_blocks, value_blocks, pos_blocks)
        )
        return result

    return fold_keys


def attend_back(
    queries,
    query_pos,
    bias_rows,
    keys_all,
    values_all,
    pos_all,
    grad_att,
    log_total,
    row_delta,
    key_rows,
):
    local_len, head_count = (queries.shape[0], queries.shape[1])
    bucket_count = bias_rows.shape[0]
    block_count = keys_all.shape[0] // key_rows
    key_blocks = keys_all.reshape(block_count, key_rows, head_count, HDIM)
    value_blocks = values_all.reshape(block_count, key_rows, head_count, HDIM)
    pos_blocks = pos_all.reshape(block_count, key_rows)

    def attend_one_block(inner, block_item):
        grad_query, grad_bias = inner
        key_block, value_block, pos_block = block_item
        bucket, probability, grad_scores = pair_terms(
            queries,
            query_pos,
            key_block,
            pos_block,
            value_block,
            grad_att,
            log_total,
            row_delta,
            bias_rows,
        )
        grad_bias = grad_bias + table_grad(bucket, grad_scores, bucket_count)
        scores_low = grad_scores.astype(jnp.bfloat16)
        grad_query = grad_query + jnp.einsum(
            "hqk,khd->qhd", scores_low, key_block, preferred_element_type=jnp.float32
        )
        grad_value = jnp.einsum(
            "hqk,qhd->khd",
            probability.astype(jnp.bfloat16),
            grad_att,
            preferred_element_type=jnp.float32,
        )
        grad_key = jnp.einsum(
            "hqk,qhd->khd", scores_low, queries, preferred_element_type=jnp.float32
        )
        return ((grad_query, grad_bias), (grad_key, grad_value))

    start_state = (
        jnp.zeros((local_len, head_count, HDIM), jnp.float32),
        jnp.zeros((bucket_count, head_count), jnp.float32),
    )
    final_state, stacked = lax.scan(
        attend_one_block, start_state, (key_blocks, value_blocks, pos_blocks)
    )
    total_keys = keys_all.shape[0]
    return (
        final_state[0],
        final_state[1],
        stacked[0].reshape(total_keys, head_count * HDIM),
        stacked[1].reshape(total_keys, head_count * HDIM),
    )


def own_share(grad_term, grad_dim):
    share_len = grad_term.shape[grad_dim] // lax.axis_size("fsdp")
    return lax.dynamic_slice_in_dim(
        grad_term, lax.axis_index("fsdp") * share_len, share_len, grad_dim
    )


def per_device(
    tokens,
    positions,
    w_query,
    w_key,
    w_value,
    w_out,
    w_in,
    w_back,
    gain_one,
    gain_two,
    bias_table,
    cotangent,
):
    micro_count = tokens.shape[0]
    head_count = w_query.shape[1] // HDIM
    head_cols = head_count * HDIM
    hidden_cols = w_in.shape[1]
    bucket_count = bias_table.shape[0] * lax.axis_size("fsdp")
    grad_wq = jnp.zeros((D, head_cols), jnp.float32)
    grad_wk = jnp.zeros((D, head_cols), jnp.float32)
    grad_wv = jnp.zeros((D, head_cols), jnp.float32)
    grad_wo = jnp.zeros((head_cols, D), jnp.float32)
    grad_wi = jnp.zeros((D, hidden_cols), jnp.float32)
    grad_wb = jnp.zeros((hidden_cols, D), jnp.float32)
    grad_table = jnp.zeros((bucket_count, head_count), jnp.float32)
    grad_gain_one = jnp.zeros((D,), jnp.float32)
    grad_gain_two = jnp.zeros((D,), jnp.float32)
    outputs = []
    input_grads = []
    for micro_step in range(micro_count):
        full_wq, full_wk, full_wv, full_wo, full_wi, full_wb, full_g1, full_g2, full_table = (
            lax.all_gather(w_query, "fsdp", axis=0, tiled=True),
            lax.all_gather(w_key, "fsdp", axis=0, tiled=True),
            lax.all_gather(w_value, "fsdp", axis=0, tiled=True),
            lax.all_gather(w_out, "fsdp", axis=1, tiled=True),
            lax.all_gather(w_in, "fsdp", axis=0, tiled=True),
            lax.all_gather(w_back, "fsdp", axis=1, tiled=True),
            lax.all_gather(gain_one, "fsdp", axis=0, tiled=True),
            lax.all_gather(gain_two, "fsdp", axis=0, tiled=True),
            lax.all_gather(bias_table, "fsdp", axis=0, tiled=True),
        )
        gain_first = full_g1.astype(jnp.float32)
        gain_second = full_g2.astype(jnp.float32)
        bias_rows = full_table.astype(jnp.float32)
        token_rows = tokens[micro_step, 0].astype(jnp.float32)
        query_pos = positions[micro_step, 0]
        scale_one = inverse_rms(token_rows)
        normed = spread_rows((token_rows * scale_one * gain_first).astype(jnp.bfloat16))
        local_len = normed.shape[0]
        key_rows = math.gcd(local_len, 256)
        queries_low = jnp.dot(normed, full_wq, preferred_element_type=jnp.float32).astype(
            jnp.bfloat16
        )
        keys_low = jnp.dot(normed, full_wk, preferred_element_type=jnp.float32).astype(jnp.bfloat16)
        values_low = jnp.dot(normed, full_wv, preferred_element_type=jnp.float32).astype(
            jnp.bfloat16
        )
        queries = queries_low.reshape(local_len, head_count, HDIM)
        start_state = (
            jnp.full((head_count, local_len), -1e30, jnp.float32),
            jnp.zeros((head_count, local_len), jnp.float32),
            jnp.zeros((head_count, local_len, HDIM), jnp.float32),
        )
        fold_keys = make_fold(queries, query_pos, bias_rows, key_rows)
        run_peak, run_total, run_acc = fold_keys(
            start_state,
            (
                lax.all_gather(keys_low, "ctx", axis=0, tiled=True),
                lax.all_gather(values_low, "ctx", axis=0, tiled=True),
                lax.all_gather(query_pos, "ctx", axis=0, tiled=True),
            ),
            jnp.int32(0),
        )
        log_total = run_peak + jnp.log(run_total)
        attended_f = jnp.transpose(run_acc / run_total[:, :, None], (1, 0, 2)).reshape(
            local_len, head_cols
        )
        attended = attended_f.astype(jnp.bfloat16)
        middle = token_rows + collect_rows(
            jnp.dot(attended, full_wo, preferred_element_type=jnp.float32)
        )
        scale_two = inverse_rms(middle)
        normed_two = spread_rows((middle * scale_two * gain_second).astype(jnp.bfloat16))
        hidden_pre = jnp.dot(normed_two, full_wi, preferred_element_type=jnp.float32)
        hidden = jax.nn.gelu(hidden_pre, approximate=False).astype(jnp.bfloat16)
        output_rows = middle + collect_rows(
            jnp.dot(hidden, full_wb, preferred_element_type=jnp.float32)
        )
        outputs.append(output_rows.astype(jnp.bfloat16))
        grad_local = cotangent[micro_step, 0]
        grad_full = spread_rows(grad_local)
        grad_wb = grad_wb + left_product(hidden, grad_full)
        grad_hidden = right_product(grad_full, full_wb)
        grad_pre = (grad_hidden * gelu_slope(hidden_pre)).astype(jnp.bfloat16)
        grad_wi = grad_wi + left_product(normed_two, grad_pre)
        grad_normed_two = collect_rows(right_product(grad_pre, full_wi))
        grad_middle, gain_part_two = norm_back(middle, scale_two, gain_second, grad_normed_two)
        grad_middle = grad_middle + grad_local.astype(jnp.float32)
        grad_gain_two = grad_gain_two + gain_part_two
        grad_mixed = spread_rows(grad_middle.astype(jnp.bfloat16))
        grad_wo = grad_wo + left_product(attended, grad_mixed)
        grad_attended = right_product(grad_mixed, full_wo).astype(jnp.bfloat16)
        row_delta = jnp.sum(
            (grad_attended.astype(jnp.float32) * attended_f).reshape(local_len, head_count, HDIM),
            axis=-1,
        ).T
        back_keys, back_values, back_pos = (
            lax.all_gather(keys_low, "ctx", axis=0, tiled=True),
            lax.all_gather(values_low, "ctx", axis=0, tiled=True),
            lax.all_gather(query_pos, "ctx", axis=0, tiled=True),
        )
        grad_att_heads = grad_attended.reshape(local_len, head_count, HDIM)
        grad_queries, table_part, grad_keys_all, grad_values_all = attend_back(
            queries,
            query_pos,
            bias_rows,
            back_keys,
            back_values,
            back_pos,
            grad_att_heads,
            log_total,
            row_delta,
            key_rows,
        )
        grad_keys, grad_values = (
            lax.psum_scatter(
                grad_keys_all.astype(jnp.bfloat16), "ctx", scatter_dimension=0, tiled=True
            ).astype(jnp.float32),
            lax.psum_scatter(
                grad_values_all.astype(jnp.bfloat16), "ctx", scatter_dimension=0, tiled=True
            ).astype(jnp.float32),
        )
        grad_table = grad_table + table_part
        grad_q_low = grad_queries.reshape(local_len, head_cols).astype(jnp.bfloat16)
        grad_k_low = grad_keys.astype(jnp.bfloat16)
        grad_v_low = grad_values.astype(jnp.bfloat16)
        grad_wq = grad_wq + left_product(normed, grad_q_low)
        grad_wk = grad_wk + left_product(normed, grad_k_low)
        grad_wv = grad_wv + left_product(normed, grad_v_low)
        grad_normed = collect_rows(
            right_product(grad_q_low, full_wq)
            + right_product(grad_k_low, full_wk)
            + right_product(grad_v_low, full_wv)
        )
        grad_input, gain_part_one = norm_back(token_rows, scale_one, gain_first, grad_normed)
        grad_gain_one = grad_gain_one + gain_part_one
        input_grads.append((grad_input + grad_middle).astype(jnp.bfloat16))
    gain_total_one, gain_total_two = lax.psum((grad_gain_one, grad_gain_two), ("fsdp", "ctx", "tp"))
    sum_wq, sum_wk, sum_wv, sum_wo, sum_wi, sum_wb, sum_table = lax.psum(
        (grad_wq, grad_wk, grad_wv, grad_wo, grad_wi, grad_wb, grad_table), ("fsdp", "ctx")
    )
    share_wq = own_share(sum_wq, 0)
    share_wk = own_share(sum_wk, 0)
    share_wv = own_share(sum_wv, 0)
    share_wo = own_share(sum_wo, 1)
    share_wi = own_share(sum_wi, 0)
    share_wb = own_share(sum_wb, 1)
    share_table = own_share(sum_table, 0)
    return (
        jnp.stack(outputs)[:, None],
        jnp.stack(input_grads)[:, None],
        own_share(gain_total_one, 0),
        own_share(gain_total_two, 0),
        share_wq,
        share_wk,
        share_wv,
        share_wo,
        share_wi,
        share_wb,
        share_table,
    )


def solution(mesh):
    return jax.shard_map(
        per_device,
        mesh=mesh,
        in_specs=(
            P(None, "fsdp", ("ctx", "tp"), None),
            P(None, "fsdp", "ctx"),
            P("fsdp", "tp"),
            P("fsdp", "tp"),
            P("fsdp", "tp"),
            P("tp", "fsdp"),
            P("fsdp", "tp"),
            P("tp", "fsdp"),
            P("fsdp"),
            P("fsdp"),
            P("fsdp", "tp"),
            P(None, "fsdp", ("ctx", "tp"), None),
        ),
        out_specs=(
            P(None, "fsdp", ("ctx", "tp"), None),
            P(None, "fsdp", ("ctx", "tp"), None),
            P("fsdp"),
            P("fsdp"),
            P("fsdp", "tp"),
            P("fsdp", "tp"),
            P("fsdp", "tp"),
            P("tp", "fsdp"),
            P("fsdp", "tp"),
            P("tp", "fsdp"),
            P("fsdp", "tp"),
        ),
        check_vma=False,
    )
```

profile of v0, /device:TPU:0, one launch (start us, length us, event | category | flops | bytes accessed | tf_op | source)
XLA Modules:
  0.0 1103.9 jit_solution(17608964833843017369)
XLA Ops:
  32.0 14.7 %all_gather.120 = bf16[1024,192]{0,1:T(8,128)(2,1)S(1)} all-gather(bf16[256,192]{0,1:T(8,128)(2,1)S(1)} %convolution_convert_fusion.20), channel_id=1, replica_groups=mesh['fsdp'=2,'ctx'=4,'tp'=4] {'ctx'}, dimensions={0}, use_global_device_ids=true | all-gather | bytes 491520 | tf_op jit(solution)/shard_map/all_gather | solution.py:273
  54.5 11.9 %all-gather = s32[1,1,1024]{2,1,0:T(1,128)S(1)} all-gather(s32[1,1,256]{2,1,0:T(1,128)} %get-tuple-element.1803), channel_id=2, replica_groups=mesh['fsdp'=2,'ctx'=4,'tp'=4] {'ctx'}, dimensions={2}, use_global_device_ids=true | all-gather | bytes 5120 | tf_op jit(solution)/shard_map/all_gather | solution.py:275
  78.6 14.3 %all_gather.125 = bf16[1024,192]{0,1:T(8,128)(2,1)S(1)} all-gather(bf16[256,192]{0,1:T(8,128)(2,1)S(1)} %convolution_convert_fusion.18), channel_id=1, replica_groups=mesh['fsdp'=2,'ctx'=4,'tp'=4] {'ctx'}, dimensions={0}, use_global_device_ids=true | all-gather | bytes 491520 | tf_op jit(solution)/shard_map/all_gather | solution.py:274
  94.1 45.2 %while.96 = (s32[]{:T(128)}, f32[3,256]{1,0:T(4,128)S(1)}, f32[3,256]{1,0:T(4,128)S(1)}, f32[3,256,64]{1,2,0:T(8,128)S(1)}, bf16[4,256,3,64]{1,3,2,0:T(8,128)(2,...) while((s32[]{:T(128)}, f32[3,256]{1,0:T(4,128)S(1)}, ...), condition=%wide.region_5.6_spmd.clone, body=%wide.region_1.5_spmd.clone.sunk | while | flops 67915520 | bytes 10965525 | solution.py:125
  154.3 15.3 %all_gather.132 = bf16[1024,192]{0,1:T(8,128)(2,1)S(1)} all-gather(bf16[256,192]{0,1:T(8,128)(2,1)S(1)} %convolution_convert_fusion.17), channel_id=1, replica_groups=mesh['fsdp'=2,'ctx'=4,'tp'=4] {'ctx'}, dimensions={0}, use_global_device_ids=true | all-gather | bytes 491520 | tf_op jit(solution)/shard_map/all_gather | solution.py:273
  179.1 14.3 %all_gather.134 = bf16[1024,192]{0,1:T(8,128)(2,1)S(1)} all-gather(bf16[256,192]{0,1:T(8,128)(2,1)S(1)} %convolution_convert_fusion.15), channel_id=1, replica_groups=mesh['fsdp'=2,'ctx'=4,'tp'=4] {'ctx'}, dimensions={0}, use_global_device_ids=true | all-gather | bytes 491520 | tf_op jit(solution)/shard_map/all_gather | solution.py:274
  194.5 44.6 %while.97 = (s32[]{:T(128)}, f32[3,256]{1,0:T(4,128)S(1)}, f32[3,256]{1,0:T(4,128)}, f32[3,256,64]{1,2,0:T(8,128)}, bf16[4,256,3,64]{1,3,2,0:T(8,128)(2,1)S(1)},...) while((s32[]{:T(128)}, f32[3,256]{1,0:T(4,128)S(1)}, ...), condition=%wide.region_14.15_spmd.clone, body=%wide.region_10.0_spmd.clone.sunk | while | flops 67915520 | bytes 10990157 | solution.py:125
  248.7 14.7 %all_gather.137 = bf16[1024,192]{0,1:T(8,128)(2,1)S(1)} all-gather(bf16[256,192]{0,1:T(8,128)(2,1)S(1)} %convolution_convert_fusion.14), channel_id=1, replica_groups=mesh['fsdp'=2,'ctx'=4,'tp'=4] {'ctx'}, dimensions={0}, use_global_device_ids=true | all-gather | bytes 491520 | tf_op jit(solution)/shard_map/all_gather | solution.py:273
  264.4 11.4 %all-gather.2 = s32[1,1,1024]{2,1,0:T(1,128)S(1)} all-gather(s32[1,1,256]{2,1,0:T(1,128)} %get-tuple-element.1851), channel_id=4, replica_groups=mesh['fsdp'=2,'ctx'=4,'tp'=4] {'ctx'}, dimensions={2}, use_global_device_ids=true | all-gather | bytes 5120 | tf_op jit(solution)/shard_map/all_gather | solution.py:275
  277.1 15.5 %all_gather.139 = bf16[1024,192]{0,1:T(8,128)(2,1)S(1)} all-gather(bf16[256,192]{0,1:T(8,128)(2,1)S(1)} %convolution_convert_fusion.12), channel_id=1, replica_groups=mesh['fsdp'=2,'ctx'=4,'tp'=4] {'ctx'}, dimensions={0}, use_global_device_ids=true | all-gather | bytes 491520 | tf_op jit(solution)/shard_map/all_gather | solution.py:274
  293.8 45.2 %while.98 = (s32[]{:T(128)}, f32[3,256]{1,0:T(4,128)S(1)}, f32[3,256]{1,0:T(4,128)S(1)}, f32[3,256,64]{1,2,0:T(8,128)S(1)}, bf16[4,256,3,64]{1,3,2,0:T(8,128)(2,...) while((s32[]{:T(128)}, f32[3,256]{1,0:T(4,128)S(1)}, ...), condition=%wide.region_23.24_spmd.clone, body=%wide.region_19.23_spmd.clone.sunk | while | flops 67915520 | bytes 10965525 | solution.py:125
  352.5 9.1 all-gather.4
  441.7 23.2 %reduce-scatter.31.cloned.1.call-done = bf16[64,768]{1,0:T(8,128)(2,1)} async-done(((bf16[256,768]{1,0:T(8,128)(2,1)}), bf16[64,768]{1,0:T(8,128)(2,1)}) %reduce-scatter.31.cloned.1.call-update) | async-done | bytes 98320 | tf_op jit(solution)/shard_map/reduce_scatter | solution.py:69
  466.9 21.4 %reduce-scatter.25.cloned.1.call-done = bf16[64,768]{1,0:T(8,128)(2,1)} async-done(((bf16[256,768]{1,0:T(8,128)(2,1)}), bf16[64,768]{1,0:T(8,128)(2,1)}) %reduce-scatter.25.cloned.1.call-update) | async-done | bytes 98320 | tf_op jit(solution)/shard_map/reduce_scatter | solution.py:69
  488.3 23.4 %reduce-scatter.21.cloned.1.call-done = bf16[64,768]{1,0:T(8,128)(2,1)} async-done(((bf16[256,768]{1,0:T(8,128)(2,1)}), bf16[64,768]{1,0:T(8,128)(2,1)}) %reduce-scatter.21.cloned.1.call-update) | async-done | bytes 98320 | tf_op jit(solution)/shard_map/reduce_scatter | solution.py:69
  523.1 85.1 %while.99 = (s32[]{:T(128)}, f32[256,3,64]{0,2,1:T(8,128)}, f32[32,3]{1,0:T(8,128)}, bf16[4,256,3,64]{1,3,2,0:T(8,128)(2,1)}, bf16[4,256,3,64]{1,3,2,0:T(8,128)(...) while((s32[]{:T(128)}, f32[256,3,64]{0,2,1:T(8,128)}, ...), condition=%wide.region_33.34_spmd.clone, body=%wide.region_30.33_spmd.clone.sunk | while | flops 158236768 | bytes 27180264 | solution.py:186
  623.8 80.6 %while.101 = (s32[]{:T(128)}, f32[256,3,64]{0,2,1:T(8,128)}, f32[32,3]{1,0:T(8,128)S(1)}, bf16[4,256,3,64]{1,3,2,0:T(8,128)(2,1)}, bf16[4,256,3,64]{1,3,2,0:T(8,...) while((s32[]{:T(128)}, f32[256,3,64]{0,2,1:T(8,128)}, ...), condition=%wide.region_55.56_spmd.clone, body=%wide.region_52.55_spmd.clone.sunk | while | flops 158236768 | bytes 27177136 | solution.py:186
  721.5 75.9 %while.100 = (s32[]{:T(128)}, f32[256,3,64]{0,2,1:T(8,128)}, f32[32,3]{1,0:T(8,128)}, bf16[4,256,3,64]{1,3,2,0:T(8,128)(2,1)}, bf16[4,256,3,64]{1,3,2,0:T(8,128)...) while((s32[]{:T(128)}, f32[256,3,64]{0,2,1:T(8,128)}, ...), condition=%wide.region_44.45_spmd.clone, body=%wide.region_41.44_spmd.clone.sunk | while | flops 158236768 | bytes 27181288 | solution.py:186
  822.9 19.0 %reduce-scatter.43.cloned.1.call-done = bf16[256,192]{0,1:T(8,128)(2,1)} async-done(((bf16[1024,192]{0,1:T(8,128)(2,1)}), bf16[256,192]{0,1:T(8,128)(2,1)}) %reduce-scatter.43.cloned.1.call-update) | async-done | bytes 98320 | tf_op jit(solution)/shard_map/reduce_scatter | solution.py:334
  848.3 19.0 %psum.71 = f32[32,3]{0,1:T(4,128)S(1)} all-reduce(f32[32,3]{0,1:T(4,128)S(1)} %add_add_fusion.4), channel_id=1, replica_groups=mesh['fsdp'=2,'ctx'=4,'tp'=4] {'fsdp','ctx'}, use_global_device_ids=true, to_apply=%region_74.75 | all-reduce | flops 96 | bytes 768 | tf_op jit(solution)/shard_map/psum | solution.py:354
  868.8 17.8 %reduce-scatter.53.cloned.1.call-done = bf16[64,768]{1,0:T(8,128)(2,1)} async-done(((bf16[256,768]{1,0:T(8,128)(2,1)}), bf16[64,768]{1,0:T(8,128)(2,1)}) %reduce-scatter.53.cloned.1.call-update) | async-done | bytes 98320 | tf_op jit(solution)/shard_map/reduce_scatter | solution.py:69
  886.6 23.2 %reduce-scatter.45.cloned.1.call-done = bf16[64,768]{1,0:T(8,128)(2,1)} async-done(((bf16[256,768]{1,0:T(8,128)(2,1)}), bf16[64,768]{1,0:T(8,128)(2,1)}) %reduce-scatter.45.cloned.1.call-update) | async-done | bytes 98320 | tf_op jit(solution)/shard_map/reduce_scatter | solution.py:69
  911.2 41.7 %all-reduce = (f32[768]{0:T(1024)S(1)}, f32[768]{0:T(1024)S(1)}) all-reduce(f32[768]{0:T(1024)S(1)} %add_add_fusion.3, f32[768]{0:T(1024)S(1)} %add_add_fusion.2), channel_id=1, replica_groups=mesh['fsdp'=2,'ctx'=4,'tp'=4] {'fsdp','ctx','tp'}, use_global_device_ids=true, to_apply=%region_63.64 | all-reduce | flops 1536 | bytes 12288 | tf_op jit(solution)/shard_map/psum | solution.py:353
  956.2 130.8 %all-reduce.4.cloned.1.call-done = (f32[768,192]{0,1:T(8,128)}, f32[768,192]{0,1:T(8,128)}, f32[768,192]{0,1:T(8,128)}, f32[192,768]{1,0:T(8,128)}, f32[768,768]{1,0:T(8,128)}, /*index=5*/f32[768,768]{1,0:T(8,128)}) async-done(((f32[768,192]{0,1:T(8,128)}, f32[768,192]{0,1:T(8,128)}, f32[768,192]{0,1:T(8,128)}, f32[192,768]{1,0:T(8,128)}, f32[768,768]{1,0:T(8,128)}, /*index=5*/f32[768,768]{1,0:T(8,128)}), ...) | async-done | bytes 7077904 | tf_op jit(solution)/shard_map/psum | solution.py:354
  (915 shorter events, 641.8 us)
Async XLA Ops:
  8.0 361.8 %reduce-scatter.19.cloned.1.call-start = ((), (), s32[]{:S(2)}) async-start(), calls=%async_computation.18 | async-start | bytes 491520 | tf_op jit(solution)/shard_map/reduce_scatter | solution.py:69
  31.7 215.9 %copy-start.8 = (bf16[768,192]{0,1:T(8,128)(2,1)}, bf16[768,192]{0,1:T(8,128)(2,1)S(1)}, u32[]{:S(2)}) copy-start(bf16[768,192]{0,1:T(8,128)(2,1)S(1)} %all_gather.119) | copy-start | bytes 884740
  53.6 194.3 %copy-start.10 = (bf16[768,192]{0,1:T(8,128)(2,1)}, bf16[768,192]{0,1:T(8,128)(2,1)S(1)}, u32[]{:S(2)}) copy-start(bf16[768,192]{0,1:T(8,128)(2,1)S(1)} %all_gather.121) | copy-start | bytes 884740
  78.3 169.9 %copy-start.12 = (bf16[768,192]{0,1:T(8,128)(2,1)}, bf16[768,192]{0,1:T(8,128)(2,1)S(1)}, u32[]{:S(2)}) copy-start(bf16[768,192]{0,1:T(8,128)(2,1)S(1)} %all_gather.124) | copy-start | bytes 884740
  146.8 223.0 %reduce-scatter.23.cloned.1.call-start = ((), (), s32[]{:S(2)}) async-start(), calls=%async_computation.22 | async-start | bytes 491520 | tf_op jit(solution)/shard_map/reduce_scatter | solution.py:69
  241.4 128.5 %reduce-scatter.27.cloned.1.call-start = ((), (), s32[]{:S(2)}) async-start(), calls=%async_computation.24 | async-start | bytes 491520 | tf_op jit(solution)/shard_map/reduce_scatter | solution.py:69
  340.1 54.4 %all-gather.12.cloned.1.call-start = ((), (), s32[]{:S(2)}) async-start(), calls=%async_computation.19 | async-start | bytes 1769472 | tf_op jit(solution)/shard_map/all_gather | solution.py:241
  340.7 55.7 %all-gather.14.cloned.1.call-start = ((), (), s32[]{:S(2)}) async-start(), calls=%async_computation.20 | async-start | bytes 1769472 | tf_op jit(solution)/shard_map/all_gather | solution.py:242
  341.3 94.6 %reduce-scatter.47.cloned.1.call-start = ((), (), s32[]{:S(2)}) async-start(), calls=%async_computation.34 | async-start | bytes 491520 | tf_op jit(solution)/shard_map/reduce_scatter | solution.py:69
  400.0 41.7 %reduce-scatter.39.cloned.1.call-start = ((), (), s32[]{:S(2)}) async-start(), calls=%async_computation.30 | async-start | bytes 491520 | tf_op jit(solution)/shard_map/reduce_scatter | solution.py:69
  406.5 58.4 %reduce-scatter.31.cloned.1.call-start = ((), (), s32[]{:S(2)}) async-start(), calls=%async_computation.26 | async-start | bytes 491520 | tf_op jit(solution)/shard_map/reduce_scatter | solution.py:69
  413.0 75.3 %reduce-scatter.25.cloned.1.call-start = ((), (), s32[]{:S(2)}) async-start(), calls=%async_computation.23 | async-start | bytes 491520 | tf_op jit(solution)/shard_map/reduce_scatter | solution.py:69
  418.4 93.3 %reduce-scatter.21.cloned.1.call-start = ((), (), s32[]{:S(2)}) async-start(), calls=%async_computation.21 | async-start | bytes 491520 | tf_op jit(solution)/shard_map/reduce_scatter | solution.py:69
  424.7 188.0 %reduce-scatter.29.cloned.1.call-start = ((), (), s32[]{:S(2)}) async-start(), calls=%async_computation.25 | async-start | bytes 491520 | tf_op jit(solution)/shard_map/reduce_scatter | solution.py:69
  429.6 378.9 %reduce-scatter.33.cloned.1.call-start = ((), (), s32[]{:S(2)}) async-start(), calls=%async_computation.27 | async-start | bytes 491520 | tf_op jit(solution)/shard_map/reduce_scatter | solution.py:331
  612.6 198.0 %reduce-scatter.35.cloned.1.call-start = ((), (), s32[]{:S(2)}) async-start(), calls=%async_computation.28 | async-start | bytes 491520 | tf_op jit(solution)/shard_map/reduce_scatter | solution.py:334
  622.1 191.1 %reduce-scatter.49.cloned.1.call-start = ((), (), s32[]{:S(2)}) async-start(), calls=%async_computation.35 | async-start | bytes 491520 | tf_op jit(solution)/shard_map/reduce_scatter | solution.py:331
  706.7 108.7 %reduce-scatter.51.cloned.1.call-start = ((), (), s32[]{:S(2)}) async-start(), calls=%async_computation.36 | async-start | bytes 491520 | tf_op jit(solution)/shard_map/reduce_scatter | solution.py:334
  719.9 100.8 %reduce-scatter.41.cloned.1.call-start = ((), (), s32[]{:S(2)}) async-start(), calls=%async_computation.31 | async-start | bytes 491520 | tf_op jit(solution)/shard_map/reduce_scatter | solution.py:331
  799.7 42.1 %reduce-scatter.43.cloned.1.call-start = ((), (), s32[]{:S(2)}) async-start(), calls=%async_computation.32 | async-start | bytes 491520 | tf_op jit(solution)/shard_map/reduce_scatter | solution.py:334
  806.8 62.0 %reduce-scatter.37.cloned.1.call-start = ((), (), s32[]{:S(2)}) async-start(), calls=%async_computation.29 | async-start | bytes 491520 | tf_op jit(solution)/shard_map/reduce_scatter | solution.py:69
  812.9 73.7 %reduce-scatter.53.cloned.1.call-start = ((), (), s32[]{:S(2)}) async-start(), calls=%async_computation.37 | async-start | bytes 491520 | tf_op jit(solution)/shard_map/reduce_scatter | solution.py:69
  817.6 92.2 %reduce-scatter.45.cloned.1.call-start = ((), (), s32[]{:S(2)}) async-start(), calls=%async_computation.33 | async-start | bytes 491520 | tf_op jit(solution)/shard_map/reduce_scatter | solution.py:69
  844.1 242.9 %all-reduce.4.cloned.1.call-start = ((), (), s32[]{:S(2)}) async-start(), calls=%async_computation.38 | async-start | bytes 14155776 | tf_op jit(solution)/shard_map/psum | solution.py:354
  (183 other events, 2730.8 us)
Sparse Core Ops, SparseCore 0:
  147.0 18.8 reduce-scatter.18
  241.5 21.1 reduce-scatter.22
  340.3 20.8 reduce-scatter.26
  400.1 18.3 reduce-scatter.46
  420.8 20.8 reduce-scatter.38
  444.0 20.8 reduce-scatter.30
  467.4 20.8 reduce-scatter.24
  490.8 20.8 reduce-scatter.20
  514.1 20.8 reduce-scatter.28
  612.7 20.8 reduce-scatter.32
  636.0 18.8 reduce-scatter.34
  706.7 20.8 reduce-scatter.48
  730.0 18.8 reduce-scatter.50
  799.8 20.8 reduce-scatter.40
  822.9 18.8 reduce-scatter.42
  844.2 19.0 reduce-scatter.36
  865.7 20.8 reduce-scatter.52
  888.9 20.8 reduce-scatter.44
Sparse Core Ops, SparseCore 1:
  342.2 20.6 all-gather.11
  364.2 22.6 all-gather.13
  850.2 236.7 all-reduce.3
where the time goes:
time: 1120 us; the launch traced here: 1100 us
  blocking collectives  301 us (27%)
  other arithmetic  277 us (25%)
  waiting for transfers between devices  269 us (24%)
  matrix products  157 us (14%)
  local copies, waits for them, and re-layouts  77.1 us (7%)
  between operations  17.7 us (2%)
    reduce_sum x24, other arithmetic, table_bias(): jnp.sum(jnp.where(matches, bias_rows.T[:, None, None, :], 0.0), axis=-1)  134 us
    psum x1, waiting for transfers between devices, per_device(): lax.psum((grad_wq, grad_wk, grad_wv, grad_wo, grad_wi, grad_wb, grad_tabl...  131 us
    reduce_scatter x12, waiting for transfers between devices, collect_rows(): lax.psum_scatter(partial_rows.astype(jnp.bfloat16), 'tp', scatter_dimensi...  115 us
    all_gather x12, blocking collectives, spread_rows(): return lax.all_gather(local_rows, 'tp', axis=0, tiled=True)  82.3 us
    reduce_sum x12, other arithmetic, table_grad(): return jnp.sum(jnp.where(matches, grad_scores[None], 0.0), axis=(2, 3))  50.6 us
    all_gather x3, blocking collectives, per_device(): lax.all_gather(keys_low, 'ctx', axis=0, tiled=True)  44.7 us
    all_gather x3, blocking collectives, per_device(): lax.all_gather(values_low, 'ctx', axis=0, tiled=True)  44.2 us
    psum x1, blocking collectives, per_device(): lax.psum((grad_gain_one, grad_gain_two), ('fsdp', 'ctx', 'tp'))  41.7 us
  transfers between devices with their start and end apart: 21, of which 9 were waited for; matrix products, arithmetic and copies ran while one was open for 39% of the time, Pallas kernels for 0%

commit v1 on v0

--- a/solution.py
+++ b/solution.py
@@ -1,8 +1,11 @@
+import functools
 import math
 
 import jax
 import jax.numpy as jnp
 from jax import lax
+from jax.experimental import pallas as pl
+from jax.experimental.pallas import tpu as pltpu
 from jax.sharding import PartitionSpec as P
 
 D = 768
@@ -202,7 +205,7 @@
     )
 
 
-def per_device(
+def per_device_plain(
     tokens,
     positions,
     w_query,
@@ -376,9 +379,933 @@
     )
 
 
+MESH = pl.DeviceIdType.MESH
+F32 = jnp.float32
+BF16 = jnp.bfloat16
+HEADS_HERE = 3
+BLK = 128
+VALUE_ROWS = (128, 192, 64)
+
+
+def nn(left, right):
+    return lax.dot_general(left, right, (((1,), (0,)), ((), ())), preferred_element_type=F32)
+
+
+def nt(left, right):
+    return lax.dot_general(left, right, (((1,), (1,)), ((), ())), preferred_element_type=F32)
+
+
+def tn(left, right):
+    return lax.dot_general(left, right, (((0,), (0,)), ((), ())), preferred_element_type=F32)
+
+
+def at_rows(offset, size, unit):
+    return pl.ds(pl.multiple_of(offset, unit), size)
+
+
+def fold_rows(block):
+    return jnp.sum(block.reshape(block.shape[0] // 8, 8, block.shape[1]), axis=0)
+
+
+class Sems:
+    def __init__(self):
+        self.numbers = {}
+
+    def __call__(self, *name):
+        return self.numbers.setdefault(name, len(self.numbers))
+
+
+def grad_chunks(share, hidden):
+    half = hidden // 2
+    chunks, row = [], 0
+    for name, rows, cols in (
+        ("back0", half, share),
+        ("back1", half, share),
+        ("in0", share, half),
+        ("in1", share, half),
+        ("out", HEADS_HERE * HDIM, share),
+        ("kv", share, 384),
+        ("q", share, 256),
+    ):
+        chunks.append((name, row, rows, cols))
+        row += rows
+    return chunks, row
+
+
+def layer_kernel(
+    nf, nc, micro, rows_own, share, hidden, n_sems, sems,
+    tok, pos_in, cot, wqkv_loc, wo_loc, wi_loc, wb_loc, small_loc,
+    out, grad_in, grads_out, small_out,
+    wqkv, wo, wi, wb, small_rx, smallf, n1, g, posb, bkt, bias, qm, kv, e_t, s_t, ds_t, att_t,
+    inv, att, scr, keep, keep6, send1, send2, recv1, recv2, zsend, zrecv, gz, n2, hid, gp, gm,
+    mid_f, gmid, dq, dom, nds, tacc, facc, gain2, xs, xr, zr1, zr2, tot, sm, smr,
+    ssem, rsem, lsem,
+):
+    f, c, t = lax.axis_index("fsdp"), lax.axis_index("ctx"), lax.axis_index("tp")
+    nt_ = 4
+    T = rows_own
+    R = nt_ * T
+    L = nc * R
+    NB = L // BLK
+    t1 = t + 1 - 2 * lax.rem(t, 2)
+    t2 = lax.rem(t + 2, 4)
+    t3 = lax.rem(t1 + 2, 4)
+    sib, ypeer = (f, c, t1), (f, c, t2)
+    xpeers = [(lax.rem(f + j, nf), c, t) for j in range(1, nf)]
+    zpeers = [(f, lax.rem(c + k, nc), t) for k in range(1, nc)]
+    half_c = nc // 2
+    low_side = c < half_c
+    inward = jnp.where(low_side, c + 1, c - 1)
+    outward = jnp.clip(jnp.where(low_side, c - 1, c + 1), 0, nc - 1)
+    is_mid = (c == half_c - 1) | (c == half_c)
+    has_out = (c > 0) & (c < nc - 1)
+    if nc == 2:
+        has_out = c < 0
+    chunks, chunk_rows = grad_chunks(share, hidden)
+    pending = []
+    zs = xs.at[0]
+
+    def send(src, dst, name_s, name_r, dev, when=None):
+        copy = pltpu.make_async_remote_copy(
+            src, dst, ssem.at[sems(*name_s)], rsem.at[sems(*name_r)], device_id=dev, device_id_type=MESH
+        )
+        if when is None:
+            copy.start()
+        else:
+            pl.when(when)(copy.start)
+        pending.append((name_s, copy, when))
+
+    def sent(*name_s):
+        for at, (name, copy, when) in enumerate(pending):
+            if name == name_s:
+                if when is None:
+                    copy.wait_send()
+                else:
+                    pl.when(when)(copy.wait_send)
+                del pending[at]
+                return
+
+    def arrived(dst, *name_r):
+        pltpu.make_async_remote_copy(
+            dst, dst, ssem.at[sems(*name_r)], rsem.at[sems(*name_r)], device_id=sib, device_id_type=MESH
+        ).wait_recv()
+
+    def rms(rows):
+        return lax.rsqrt(jnp.mean(rows * rows, axis=-1, keepdims=True) + epsilon)
+
+    def piece(buf, m, block, t_of):
+        return buf.at[m, at_rows(block * R + t_of * T, T, T)]
+
+    for m in range(micro):
+        rows = tok[m].astype(F32)
+        n1[m, at_rows(c * R + t * T, T, T)] = (rows * rms(rows)).astype(BF16)
+    dom[...] = jnp.zeros_like(dom)
+    tacc[...] = jnp.zeros_like(tacc)
+    facc[...] = jnp.zeros_like(facc)
+    posb[0] = jnp.zeros_like(posb[0])
+    posb[2] = jnp.zeros_like(posb[2])
+    posb[1] = pos_in[...]
+    local = []
+
+    def local_copy(src, dst, i):
+        copy = pltpu.make_async_copy(src, dst, lsem.at[i])
+        copy.start()
+        local.append(copy)
+
+    share_cols = at_rows(f * share, share, BLK)
+    share_rows = at_rows(f * share, share, BLK)
+    own_rows = at_rows(t * T, T, T)
+    local_copy(wo_loc.at[pl.ds(0, 128)], wo.at[pl.ds(128, 128), share_cols], 0)
+    local_copy(wo_loc.at[pl.ds(128, 64)], wo.at[pl.ds(64, 64), share_cols], 1)
+    local_copy(wi_loc, wi.at[share_rows], 2)
+    local_copy(wb_loc, wb.at[:, share_cols], 3)
+    for m in range(micro):
+        local_copy(cot.at[m], g.at[m, own_rows], 4 + m)
+    wo[pl.ds(0, 64)] = jnp.zeros((64, D), BF16)
+
+    barrier = pltpu.get_barrier_semaphore()
+    peers = [sib, ypeer] + xpeers + zpeers
+    for dev in peers:
+        pl.semaphore_signal(barrier, inc=1, device_id=dev, device_id_type=MESH)
+    pl.semaphore_wait(barrier, len(peers))
+
+    def spread_first(m):
+        mine = piece(n1, m, c, t)
+        send(mine, mine, ("ny", m, 0), ("ny", m, 0), ypeer)
+        for k in range(1, nc):
+            send(mine, mine, ("nz", m, k), ("nz", m, nc - k), zpeers[k - 1])
+        send(mine, mine, ("ns", m, 0), ("ns", m, 0), sib)
+
+    spread_first(0)
+    for j, dev in enumerate(xpeers):
+        send(wqkv_loc, wqkv.at[share_rows], ("wqkv", j), ("wqkv", nf - 2 - j), dev)
+        send(small_loc, small_rx.at[f], ("small", j), ("small", nf - 2 - j), dev)
+    send(pos_in, posb.at[0], ("posu",), ("posu",), (f, jnp.minimum(c + 1, nc - 1), t), c < nc - 1)
+    send(pos_in, posb.at[2], ("posd",), ("posd",), (f, jnp.maximum(c - 1, 0), t), c > 0)
+    for m in range(1, micro):
+        spread_first(m)
+    for j, dev in enumerate(xpeers):
+        send(wo_loc.at[pl.ds(0, 128)], wo.at[pl.ds(128, 128), share_cols], ("woa", j), ("woa", nf - 2 - j), dev)
+        send(wo_loc.at[pl.ds(128, 64)], wo.at[pl.ds(64, 64), share_cols], ("wob", j), ("wob", nf - 2 - j), dev)
+        send(wi_loc, wi.at[share_rows], ("wi", j), ("wi", nf - 2 - j), dev)
+        send(wb_loc, wb.at[:, share_cols], ("wb", j), ("wb", nf - 2 - j), dev)
+    wqkv[share_rows] = wqkv_loc[...]
+    small_rx[f] = small_loc[...]
+
+    def spread_own(name, buf, m):
+        mine = buf.at[m, own_rows]
+        send(mine, mine, (name, "y", m), (name, "y", m), ypeer)
+        send(mine, mine, (name, "s", m), (name, "s", m), sib)
+
+    def spread_on(name, buf, m):
+        there = buf.at[m, at_rows(t2 * T, T, T)]
+        arrived(there, name, "y", m)
+        send(there, there, (name, "f", m), (name, "f", m), sib)
+
+    def spread_end(name, buf, m):
+        arrived(buf.at[m, at_rows(t1 * T, T, T)], name, "s", m)
+        arrived(buf.at[m, at_rows(t3 * T, T, T)], name, "f", m)
+
+    def gather_z(m, k):
+        z = lax.rem(c + k, nc)
+        there = piece(n1, m, z, t)
+        arrived(there, "nz", m, k)
+        send(there, there, ("ny", m, k), ("ny", m, k), ypeer)
+        send(there, there, ("ns", m, k), ("ns", m, k), sib)
+
+    def gather_y(m, k):
+        z = lax.rem(c + k, nc)
+        there = piece(n1, m, z, t2)
+        arrived(there, "ny", m, k)
+        send(there, there, ("nf", m, k), ("nf", m, k), sib)
+
+    order = [k for pair in zip(range(1, nc), range(nc - 1, 0, -1)) for k in pair]
+    order = list(dict.fromkeys(order))
+
+    def gather(m):
+        gather_y(m, 0)
+        for at, k in enumerate(order):
+            gather_z(m, k)
+            if at >= 1:
+                gather_y(m, order[at - 1])
+        gather_y(m, order[-1])
+
+    def gather_end(m):
+        for k in range(nc):
+            z = lax.rem(c + k, nc)
+            arrived(piece(n1, m, z, t1), "ns", m, k)
+            arrived(piece(n1, m, z, t3), "nf", m, k)
+
+    def take_small():
+        for j in range(nf - 1):
+            arrived(small_rx.at[lax.rem(f + 1 + j, nf)], "small", j)
+        total = small_rx[0]
+        for j in range(1, nf):
+            total = total + small_rx[j]
+        smallf[...] = total
+
+    def positions_and_bias():
+        @pl.when(c > 0)
+        def _():
+            arrived(posb.at[0], "posu")
+
+        @pl.when(c < nc - 1)
+        def _():
+            arrived(posb.at[2], "posd")
+
+        def one(m, unused):
+            for qb in range(2):
+                query_row = posb[1, m, qb : qb + 1, :]
+                for d in (-1, 0, 1):
+                    slot, row = ((0, 1), (1, 0), (1, 1), (2, 0))[qb + d + 1]
+                    key_row = posb[slot, m, row : row + 1, :]
+                    key_col = jnp.transpose(jnp.broadcast_to(key_row, (BLK, BLK)))
+                    relative = key_col - query_row
+                    size = jnp.abs(relative)
+                    bucket = jnp.minimum(size, 8)
+                    for edge_value in bucket_edges:
+                        bucket = bucket + (size >= edge_value).astype(jnp.int32)
+                    bucket = bucket + 16 * (relative > 0).astype(jnp.int32)
+                    sub = qb * 3 + d + 1
+                    bkt[m, sub] = bucket
+                    for h in range(HEADS_HERE):
+                        row_of = jnp.broadcast_to(smallf[h : h + 1, pl.ds(D, 128)], (BLK, BLK))
+                        bias[m, sub, h] = jnp.take_along_axis(row_of, bucket, axis=1).astype(BF16)
+            return unused
+
+        lax.fori_loop(0, micro, one, 0)
+
+    def fold_gain():
+        for j in range(nf - 1):
+            peer = lax.rem(f + 1 + j, nf)
+            arrived(wqkv.at[at_rows(peer * share, share, BLK)], "wqkv", j)
+
+        def one(i, unused):
+            r = at_rows(i * BLK, BLK, BLK)
+            col = jnp.transpose(jnp.broadcast_to(smallf[0:1, r], (BLK, BLK)))
+            for j in range(5):
+                cols = pl.ds(j * BLK, BLK)
+                wqkv[r, cols] = (wqkv[r, cols].astype(F32) * col).astype(BF16)
+            return unused
+
+        lax.fori_loop(0, D // BLK, one, 0)
+
+    def reduce_start(slot, rid, kept, value, previous):
+        scr[...] = value
+        if previous is not None:
+            sent("r1", previous)
+        send1[slot, 0] = scr[at_rows(t1 * T, T, T)].astype(BF16)
+        send1[slot, 1] = scr[at_rows(t3 * T, T, T)].astype(BF16)
+        send(send1.at[slot], recv1.at[rid], ("r1", rid), ("r1", rid), sib)
+        kept[0] = scr[own_rows].astype(kept.dtype)
+        kept[1] = scr[at_rows(t2 * T, T, T)].astype(kept.dtype)
+
+    def reduce_mid(slot, rid, kept, previous):
+        arrived(recv1.at[rid], "r1", rid)
+        if previous is not None:
+            sent("r2", previous)
+        send2[slot] = (kept[1].astype(F32) + recv1[rid, 1].astype(F32)).astype(BF16)
+        send(send2.at[slot], recv2.at[rid], ("r2", rid), ("r2", rid), ypeer)
+        kept[0] = (kept[0].astype(F32) + recv1[rid, 0].astype(F32)).astype(kept.dtype)
+
+    def reduce_end(rid, kept):
+        arrived(recv2.at[rid], "r2", rid)
+        return kept[0].astype(F32) + recv2[rid].astype(F32)
+
+    def phase(p, m):
+        rid = p * micro + m
+        return p, rid, keep.at[rid], (rid - 1 if m > 0 else None)
+
+    def start_phase(p, m, value):
+        slot, rid, kept, previous = phase(p, m)
+        reduce_start(slot, rid, kept, value, previous)
+
+    def mid_phase(p, m):
+        slot, rid, kept, previous = phase(p, m)
+        reduce_mid(slot, rid, kept, previous)
+
+    def end_phase(p, m):
+        slot, rid, kept, previous = phase(p, m)
+        return reduce_end(rid, kept)
+
+    def attend(m):
+        own = at_rows(c * R, R, R)
+        queries = nn(n1[m, own], wqkv[:, 0:256])
+        lane = lax.broadcasted_iota(jnp.int32, (R, 256), 1)
+        for h in range(HEADS_HERE):
+            keep_it = (lane >= h * HDIM) & (lane < (h + 1) * HDIM)
+            qm[m, pl.ds(h * R, R)] = jnp.where(keep_it, queries, 0.0).astype(BF16)
+
+        def one_block(z, unused):
+            r = at_rows(z * R, R, R)
+            kv[m, r] = nn(n1[m, r], wqkv[:, 256:640]).astype(BF16)
+            return unused
+
+        lax.fori_loop(0, nc, one_block, 0)
+        for h in range(HEADS_HERE):
+            cols = pl.ds(h * R, R)
+            below = smallf[h : h + 1, pl.ds(D, 128)][:, 15:16]
+            above = smallf[h : h + 1, pl.ds(D, 128)][:, 31:32]
+
+            def scores(kb, unused):
+                r = at_rows(kb * BLK, BLK, BLK)
+                block = nt(kv[m, r, 0:256], qm[m, cols])
+                for qb in range(2):
+                    d = kb - 2 * c - qb
+                    far = jnp.where(d < -1, below, jnp.where(d > 1, above, 0.0))
+                    s_t[r, pl.ds(qb * BLK, BLK)] = block[:, qb * BLK : (qb + 1) * BLK] + far
+                return unused
+
+            lax.fori_loop(0, NB, scores, 0)
+            for qb in range(2):
+                for d in (-1, 0, 1):
+                    kb = 2 * c + qb + d
+
+                    def near(kb=kb, qb=qb, d=d):
+                        r = at_rows(kb * BLK, BLK, BLK)
+                        q = pl.ds(qb * BLK, BLK)
+                        s_t[r, q] = s_t[r, q] + bias[m, qb * 3 + d + 1, h].astype(F32)
+
+                    if qb + d in (0, 1):
+                        near()
+                    else:
+                        pl.when((kb >= 0) & (kb < NB))(near)
+
+            def peak(kb, top):
+                block = s_t[at_rows(kb * BLK, BLK, BLK)]
+                return jnp.maximum(top, jnp.max(block.reshape(BLK // 8, 8, R), axis=0))
+
+            top = lax.fori_loop(0, NB, peak, jnp.full((8, R), -jnp.inf, F32))
+            top = jnp.max(top, axis=0, keepdims=True)
+
+            def expo(kb, total):
+                r = at_rows(kb * BLK, BLK, BLK)
+                weights = jnp.exp(s_t[r] - top)
+                e_t[m, r, cols] = weights.astype(BF16)
+                return total + fold_rows(weights)
+
+            total = lax.fori_loop(0, NB, expo, jnp.zeros((8, R), F32))
+            over = 1.0 / jnp.sum(total, axis=0, keepdims=True)
+            inv[m * HEADS_HERE + h] = jnp.broadcast_to(over, (8, R))
+            mixed = tn(kv[m, :, 128:384], e_t[m, :, cols])
+            v0 = VALUE_ROWS[h]
+            att_t[m, pl.ds(v0, HDIM)] = mixed[v0 : v0 + HDIM] * over
+        att_t[m, pl.ds(0, HDIM)] = jnp.zeros((HDIM, R), F32)
+        attended = jnp.transpose(att_t[m]).astype(BF16)
+        att[pl.ds(m * R, R)] = attended
+        return attended
+
+    def attend_and_mix(m):
+        attended = attend(m)
+        start_phase(0, m, nn(attended, wo[...]))
+
+    def take_wo():
+        local[0].wait()
+        local[1].wait()
+        for j in range(nf - 1):
+            cols = at_rows(lax.rem(f + 1 + j, nf) * share, share, BLK)
+            arrived(wo.at[pl.ds(128, 128), cols], "woa", j)
+            arrived(wo.at[pl.ds(64, 64), cols], "wob", j)
+
+    def take_ff():
+        local[2].wait()
+        local[3].wait()
+        for j in range(nf - 1):
+            peer = at_rows(lax.rem(f + 1 + j, nf) * share, share, BLK)
+            arrived(wi.at[peer], "wi", j)
+            arrived(wb.at[:, peer], "wb", j)
+
+    def norm_two(m):
+        middle = tok[m].astype(F32) + end_phase(0, m)
+        mid_f[m] = middle
+        n2[m, own_rows] = (middle * rms(middle) * smallf[1:2, 0:D]).astype(BF16)
+        spread_own("n2", n2, m)
+
+    def feed(m):
+        spread_end("n2", n2, m)
+        rows = n2[m]
+
+        def one(i, unused):
+            cols = at_rows(i * 256, 256, 256)
+            pre = nn(rows, wi[:, cols])
+            slope = nt(g[m], wb[cols])
+            bell = 0.5 * (1.0 + lax.erf(pre * 0.7071067811865476))
+            hid[m, :, cols] = (pre * bell).astype(BF16)
+            bell = bell + pre * jnp.exp(-0.5 * pre * pre) * 0.3989422804014327
+            gp[m, :, cols] = (slope * bell).astype(BF16)
+            return unused
+
+        lax.fori_loop(0, hidden // 256, one, 0)
+        start_phase(1, m, nt(gp[m], wi[...]))
+        start_phase(2, m, nn(hid[m], wb[...]))
+
+    def output_rows(m):
+        out[m] = (mid_f[m] + end_phase(2, m)).astype(BF16)
+
+    def back_two(m):
+        grad_normed = end_phase(1, m)
+        middle = mid_f[m]
+        scale = rms(middle)
+        unit = middle * scale
+        part = fold_rows(grad_normed * unit)
+        gain2[...] = part if m == 0 else gain2[...] + part
+        weighted = smallf[1:2, 0:D] * grad_normed
+        grad = scale * (weighted - unit * jnp.mean(unit * weighted, axis=-1, keepdims=True))
+        grad = grad + g[m, own_rows].astype(F32)
+        gmid[m] = grad
+        gm[m, own_rows] = grad.astype(BF16)
+        spread_own("gm", gm, m)
+
+    def attend_back(m):
+        spread_end("gm", gm, m)
+        grad_att = nt(wo[...], gm[m]).astype(BF16).astype(F32)
+        deltas = []
+        for h in range(HEADS_HERE):
+            v0 = VALUE_ROWS[h]
+            scaled = (grad_att[v0 : v0 + HDIM] * inv[m * HEADS_HERE + h, 0:1, :]).astype(BF16)
+            dom[pl.ds(v0, HDIM), pl.ds(h * R, R)] = scaled
+            deltas.append(jnp.sum(scaled.astype(F32) * att_t[m, pl.ds(v0, HDIM)], axis=0, keepdims=True))
+
+        def one_block(kb, unused):
+            r = at_rows(kb * BLK, BLK, BLK)
+            for h in range(HEADS_HERE):
+                cols = pl.ds(h * R, R)
+                grad_prob = nn(kv[m, r, 128:384], dom[:, cols])
+                grad = e_t[m, r, cols].astype(F32) * (grad_prob - deltas[h])
+                ds_t[r, cols] = grad.astype(BF16)
+                part = fold_rows(grad)
+                rel = kb - 2 * c + 1
+                low, high = part[:, 0:BLK], part[:, BLK:]
+                facc[h, 0] += jnp.where(rel < 0, low, 0.0) + jnp.where(rel < 1, high, 0.0)
+                facc[h, 1] += jnp.where(rel > 2, low, 0.0) + jnp.where(rel > 3, high, 0.0)
+
+                @pl.when((rel >= 0) & (rel < 4))
+                def _():
+                    nds[jnp.clip(rel, 0, 3), :, cols] = grad
+
+            return unused
+
+        lax.fori_loop(0, NB, one_block, 0)
+        columns = []
+        for h in range(HEADS_HERE):
+            grad_q = tn(kv[m, :, 0:256], ds_t[:, pl.ds(h * R, R)])
+            columns.append(grad_q[h * HDIM : (h + 1) * HDIM])
+        columns.append(jnp.zeros((HDIM, R), F32))
+        dq[m] = jnp.transpose(jnp.concatenate(columns, axis=0)).astype(BF16)
+
+        def one_grad(z, unused):
+            r = at_rows(z * R, R, R)
+            grad_k = nn(ds_t[r], qm[m])
+            grad_v = nt(e_t[m, r], dom[...])
+            kv[m, r, 0:128] = grad_k[:, 0:128].astype(BF16)
+            kv[m, r, 128:256] = (grad_k[:, 128:256] + grad_v[:, 0:128]).astype(BF16)
+            kv[m, r, 256:384] = grad_v[:, 128:256].astype(BF16)
+            return unused
+
+        lax.fori_loop(0, nc, one_grad, 0)
+
+    def bin_table(m):
+        for qb in range(2):
+            for d in (-1, 0, 1):
+                rel = qb + d + 1
+                sub = qb * 3 + d + 1
+
+                def one(b, unused, rel=rel, sub=sub, qb=qb):
+                    same = bkt[m, sub] == b
+                    for h in range(HEADS_HERE):
+                        block = nds[rel, :, pl.ds(h * R + qb * BLK, BLK)]
+                        tacc[h, b] += fold_rows(jnp.where(same, block, 0.0))
+                    return unused
+
+                first, last = {-1: (1, 16), 0: (0, 32), 1: (17, 32)}[d]
+
+                def run(first=first, last=last, one=one):
+                    lax.fori_loop(first, last, one, 0)
+
+                if rel in (1, 2):
+                    run()
+                else:
+                    pl.when((2 * c + rel - 1 >= 0) & (2 * c + rel - 1 < NB))(run)
+
+    def six(m, k):
+        return 3 + k, 3 * micro + m * nc + k, keep6.at[m * nc + k], (3 * micro + (m - 1) * nc + k if m > 0 else None)
+
+    def back_start(m, k):
+        r = at_rows(lax.rem(c + k, nc) * R, R, R)
+        value = nt(kv[m, r], wqkv[:, 256:640])
+        if k == 0:
+            value = value + nt(dq[m], wqkv[:, 0:256])
+        slot, rid, kept, previous = six(m, k)
+        reduce_start(slot, rid, kept, value, previous)
+
+    def back_mid(m, k):
+        slot, rid, kept, previous = six(m, k)
+        reduce_mid(slot, rid, kept, previous)
+
+    def back_out(m, k):
+        slot, rid, kept, previous = six(m, k)
+        total = reduce_end(rid, kept)
+        if k == 0:
+            gz[m] = total
+        else:
+            zsend[m, k - 1] = total.astype(BF16)
+            send(zsend.at[m, k - 1], zrecv.at[m, nc - k - 1], ("gz", m, k), ("gz", m, nc - k), zpeers[k - 1])
+
+    def back_one(m):
+        weighted = gz[m]
+        for k in range(1, nc):
+            arrived(zrecv.at[m, k - 1], "gz", m, k)
+            weighted = weighted + zrecv[m, k - 1].astype(F32)
+        rows = tok[m].astype(F32)
+        scale = rms(rows)
+        unit = rows * scale
+        grad = scale * (weighted - unit * jnp.mean(unit * weighted, axis=-1, keepdims=True))
+        grad_in[m] = (gmid[m] + grad).astype(BF16)
+
+    all_rows = micro * R
+
+    def grad_of(name, part, i):
+        r = at_rows(i * BLK, BLK, BLK)
+        share_at = at_rows(part, share, BLK)
+        if name in ("back0", "back1"):
+            at = at_rows(int(name[-1]) * (hidden // 2) + i * BLK, BLK, BLK)
+            return sum(tn(hid[m, :, at], g[m, :, share_at]) for m in range(micro))
+        if name in ("in0", "in1"):
+            at = at_rows(part + i * BLK, BLK, BLK)
+            cols = pl.ds(int(name[-1]) * (hidden // 2), hidden // 2)
+            return sum(tn(n2[m, :, at], gp[m, :, cols]) for m in range(micro))
+        at = at_rows(part + i * BLK, BLK, BLK)
+        if name == "kv":
+            return sum(tn(n1[m, :, at], kv[m]) for m in range(micro))
+        own = at_rows(c * R, R, R)
+        return sum(tn(n1[m, own, at], dq[m]) for m in range(micro))
+
+    def out_grad(part):
+        share_at = at_rows(part, share, BLK)
+        return [
+            sum(
+                tn(att[pl.ds(m * R, R), pl.ds(at, size)], gm[m, :, share_at]) for m in range(micro)
+            )
+            for at, size in ((128, 128), (64, 64))
+        ]
+
+    def each_part(chunk, part, use):
+        name, row, rows, cols = chunk
+        if name == "out":
+            first, second = out_grad(part)
+            use(row, 128, first)
+            use(row + 128, 64, second)
+            return
+
+        def one(i, unused):
+            use(pl.multiple_of(row + i * BLK, 64), BLK, grad_of(name, part, i))
+            return unused
+
+        lax.fori_loop(0, rows // BLK, one, 0)
+
+    def share_out(q):
+        chunk = chunks[q]
+        name, row, rows, cols = chunk
+        for j, dev in enumerate(xpeers):
+            part = lax.rem(f + 1 + j, nf) * share
+
+            def use(at, size, value, j=j):
+                xs[j, pl.ds(at, size), 0:cols] = value.astype(BF16)
+
+            each_part(chunk, part, use)
+            src = xs.at[j, pl.ds(row, rows), pl.ds(0, cols)]
+            dst = xr.at[nf - 2 - j, pl.ds(row, rows), pl.ds(0, cols)]
+            send(src, dst, ("x", q, j), ("x", q, nf - 2 - j), dev)
+
+    def own_share(q):
+        chunk = chunks[q]
+        name, row, rows, cols = chunk
+        for j in range(nf - 1):
+            arrived(xr.at[j, pl.ds(row, rows), pl.ds(0, cols)], "x", q, j)
+        sent("x", q, 0)
+
+        def use(at, size, value):
+            for j in range(nf - 1):
+                value = value + xr[j, pl.ds(at, size), 0:cols].astype(F32)
+            zs[pl.ds(at, size), 0:cols] = value.astype(BF16)
+            if name in ("q", "kv"):
+                i = pl.multiple_of(at - row, BLK)
+                first = 0 if name == "q" else 256
+                weight = wqkv_loc[pl.ds(i, BLK), pl.ds(first, cols)].astype(F32)
+                column = jnp.sum(weight * value, axis=1, keepdims=True)
+                line = jnp.transpose(jnp.broadcast_to(column, (BLK, BLK)))[0:1, :]
+                sm[0, 0:1, at_rows(f * share + i, BLK, BLK)] += line
+
+        each_part(chunk, f * share, use)
+
+    def ends_inward(q):
+        name, row, rows, cols = chunks[q]
+        at = (pl.ds(row, rows), pl.ds(0, cols))
+
+        @pl.when(has_out)
+        def _():
+            arrived(zr1.at[at], "zi", q)
+            zs[at] = (zs[at].astype(F32) + zr1[at].astype(F32)).astype(BF16)
+
+    def first_inward(q):
+        own_share(q)
+        name, row, rows, cols = chunks[q]
+        at = (pl.ds(row, rows), pl.ds(0, cols))
+        end = jnp.logical_not(has_out)
+        dev = (f, inward, t)
+        if nc == 2:
+            send(zs.at[at], zr2.at[at], ("ze", q), ("zx", q), dev)
+        else:
+            send(zs.at[at], zr1.at[at], ("ze", q), ("zi", q), dev, end)
+
+    def then_inward(q):
+        if nc == 2:
+            return
+        name, row, rows, cols = chunks[q]
+        at = (pl.ds(row, rows), pl.ds(0, cols))
+        ends_inward(q)
+        dev = (f, inward, t)
+        send(zs.at[at], zr2.at[at], ("zm", q), ("zx", q), dev, is_mid)
+        if nc > 4:
+            send(zs.at[at], zr1.at[at], ("zn", q), ("zi", q), dev, has_out & jnp.logical_not(is_mid))
+
+    def then_outward(q):
+        name, row, rows, cols = chunks[q]
+        at = (pl.ds(row, rows), pl.ds(0, cols))
+
+        @pl.when(is_mid)
+        def _():
+            arrived(zr2.at[at], "zx", q)
+            tot[at] = (zs[at].astype(F32) + zr2[at].astype(F32)).astype(BF16)
+
+        @pl.when(jnp.logical_not(is_mid))
+        def _():
+            arrived(tot.at[at], "zo", q)
+
+        if nc > 2:
+            send(tot.at[at], tot.at[at], ("zo", q), ("zo", q), (f, outward, t), has_out)
+        local_copy(tot.at[at], grads_out.at[at], 4 + micro + q)
+
+    def small_start():
+        g2 = jnp.sum(gain2[...], axis=0, keepdims=True)
+        sm[0, 1:2, 0:D] = g2
+        for h in range(HEADS_HERE):
+            below = jnp.sum(facc[h, 0])
+            above = jnp.sum(facc[h, 1])
+            per = jnp.sum(tacc[h], axis=1)
+            per = jnp.sum(jnp.concatenate([per, jnp.zeros((96, 128), F32)], axis=0), axis=1, keepdims=True)
+            line = jnp.transpose(jnp.broadcast_to(per, (128, 128)))[0:1, :]
+            lane = lax.broadcasted_iota(jnp.int32, (1, 128), 1)
+            line = line + jnp.where(lane == 15, below, 0.0) + jnp.where(lane == 31, above, 0.0)
+            sm[0, h : h + 1, pl.ds(D, 128)] = line
+
+    def small_send(step):
+        if step == 0:
+            send(sm.at[0], smr.at[0], ("m", 0), ("m", 0), sib)
+        elif step == 1:
+            send(sm.at[1], smr.at[1], ("m", 1), ("m", 1), ypeer)
+        elif step == 2:
+            for j, dev in enumerate(xpeers):
+                send(sm.at[2], smr.at[2 + nf - 2 - j], ("mx", j), ("mx", nf - 2 - j), dev)
+        else:
+            for k in range(1, nc):
+                send(sm.at[3], smr.at[1 + nf + nc - k - 1], ("mz", k), ("mz", nc - k), zpeers[k - 1])
+
+    def small_take(step):
+        if step < 2:
+            arrived(smr.at[step], "m", step)
+            lanes = lax.broadcasted_iota(jnp.int32, (8, D + 128), 1)
+            sm[step + 1] = sm[step] + jnp.where(lanes < D, smr[step], 0.0)
+        elif step == 2:
+            total = sm[2]
+            for j in range(nf - 1):
+                arrived(smr.at[2 + j], "mx", j)
+                total = total + smr[2 + j]
+            sm[3] = total
+        else:
+            total = sm[3]
+            for k in range(1, nc):
+                arrived(smr.at[1 + nf + k - 1], "mz", k)
+                total = total + smr[1 + nf + k - 1]
+            small_out[...] = total
+
+    sm[0] = jnp.zeros((8, D + 128), F32)
+    take_small()
+    positions_and_bias()
+    gather(0)
+    fold_gain()
+    gather_end(0)
+    take_wo()
+    for m in range(micro):
+        local[4 + m].wait()
+        spread_own("g", g, m)
+    attend_and_mix(0)
+    gather(1)
+    mid_phase(0, 0)
+    gather_end(1)
+    attend_and_mix(1)
+    norm_two(0)
+    gather(2)
+    mid_phase(0, 1)
+    spread_on("n2", n2, 0)
+    gather_end(2)
+    attend_and_mix(2)
+    norm_two(1)
+    for m in range(micro):
+        spread_on("g", g, m)
+    for m in range(micro):
+        spread_end("g", g, m)
+    take_ff()
+    feed(0)
+    mid_phase(0, 2)
+    spread_on("n2", n2, 1)
+    mid_phase(1, 0)
+    mid_phase(2, 0)
+    norm_two(2)
+    feed(1)
+    back_two(0)
+    spread_on("n2", n2, 2)
+    mid_phase(1, 1)
+    mid_phase(2, 1)
+    output_rows(0)
+    spread_on("gm", gm, 0)
+    feed(2)
+    back_two(1)
+    mid_phase(1, 2)
+    mid_phase(2, 2)
+    output_rows(1)
+    spread_on("gm", gm, 1)
+    attend_back(0)
+    back_two(2)
+    for k in range(nc):
+        back_start(0, k)
+    share_out(0)
+    spread_on("gm", gm, 2)
+    for k in range(nc):
+        back_mid(0, k)
+    bin_table(0)
+    output_rows(2)
+    attend_back(1)
+    for k in range(nc):
+        back_out(0, k)
+    for k in range(nc):
+        back_start(1, k)
+    share_out(1)
+    share_out(2)
+    for k in range(nc):
+        back_mid(1, k)
+    bin_table(1)
+    first_inward(0)
+    attend_back(2)
+    for k in range(nc):
+        back_out(1, k)
+    for k in range(nc):
+        back_start(2, k)
+    share_out(5)
+    share_out(6)
+    for k in range(nc):
+        back_mid(2, k)
+    back_one(0)
+    share_out(3)
+    share_out(4)
+    bin_table(2)
+    small_start()
+    for k in range(nc):
+        back_out(2, k)
+    first_inward(5)
+    first_inward(6)
+    small_send(0)
+    back_one(1)
+    then_inward(0)
+    first_inward(1)
+    first_inward(2)
+    small_take(0)
+    small_send(1)
+    first_inward(3)
+    first_inward(4)
+    then_inward(5)
+    then_inward(6)
+    small_take(1)
+    small_send(2)
+    back_one(2)
+    then_outward(0)
+    then_inward(1)
+    small_take(2)
+    small_send(3)
+    then_inward(2)
+    then_inward(3)
+    then_inward(4)
+    then_outward(5)
+    then_outward(6)
+    then_outward(1)
+    then_outward(2)
+    then_outward(3)
+    then_outward(4)
+    small_take(3)
+    for copy in local[4 + micro :]:
+        copy.wait()
+    for name, copy, when in pending:
+        if when is None:
+            copy.wait_send()
+        else:
+            pl.when(when)(copy.wait_send)
+    assert len(sems.numbers) <= n_sems, len(sems.numbers)
+
+
+def kernel_scratch(nf, nc, micro, T, share, hidden, n_sems):
+    R = 4 * T
+    L = nc * R
+    vm = lambda shape, kind=BF16: pltpu.VMEM(shape, kind)
+    rids = 3 * micro + nc * micro
+    chunks, chunk_rows = grad_chunks(share, hidden)
+    wide = max(384, share)
+    return [
+        vm((D, 640)), vm((256, D)), vm((D, hidden)), vm((hidden, D)),
+        vm((nf, 8, D + 128), F32), vm((8, D + 128), F32),
+        vm((micro, L, D)), vm((micro, R, D)),
+        vm((3, micro, 8, 128), jnp.int32), vm((micro, 6, BLK, BLK), jnp.int32),
+        vm((micro, 6, HEADS_HERE, BLK, BLK)),
+        vm((micro, HEADS_HERE * R, 256)), vm((micro, L, 384)),
+        vm((micro, L, HEADS_HERE * R)), vm((L, R), F32), vm((L, HEADS_HERE * R)),
+        vm((micro, 256, R), F32), vm((micro * HEADS_HERE, 8, R), F32), vm((micro * R, 256)),
+        vm((R, D), F32), vm((3 * micro, 2, T, D), F32), vm((nc * micro, 2, T, D)),
+        vm((3 + nc, 2, T, D)), vm((3 + nc, T, D)), vm((rids, 2, T, D)), vm((rids, T, D)),
+        vm((micro, nc - 1, T, D)), vm((micro, nc - 1, T, D)), vm((micro, T, D), F32),
+        vm((micro, R, D)), vm((micro, R, hidden)), vm((micro, R, hidden)), vm((micro, R, D)),
+        vm((micro, T, D), F32), vm((micro, T, D), F32), vm((micro, R, 256)),
+        vm((256, HEADS_HERE * R)), vm((4, BLK, HEADS_HERE * R), F32),
+        vm((HEADS_HERE, 32, 8, 128), F32), vm((HEADS_HERE, 2, 8, 128), F32), vm((8, D), F32),
+        vm((nf - 1, chunk_rows, wide)), vm((nf - 1, chunk_rows, wide)),
+        vm((chunk_rows, wide)), vm((chunk_rows, wide)), vm((chunk_rows, wide)),
+        vm((4, 8, D + 128), F32), vm((1 + nf + nc - 1, 8, D + 128), F32),
+        pltpu.SemaphoreType.DMA((n_sems,)), pltpu.SemaphoreType.DMA((n_sems,)),
+        pltpu.SemaphoreType.DMA((4 + micro + len(chunks),)),
+    ]
+
+
+def per_device(
+    nf, nc,
+    tokens, positions, w_query, w_key, w_value, w_out, w_in, w_back, gain_one, gain_two, bias_table, cotangent,
+):
+    micro, T = tokens.shape[0], tokens.shape[2]
+    share, hidden = w_in.shape
+    R = 4 * T
+    buckets_here = bias_table.shape[0]
+    f = lax.axis_index("fsdp")
+    wqkv = jnp.concatenate(
+        [w_query, jnp.zeros((share, 64), BF16), w_key, w_value[:, 128:], w_value[:, :128]], axis=1
+    )
+    pos = jnp.pad(positions.reshape(micro, R // 128, 128), ((0, 0), (0, 8 - R // 128), (0, 0)))
+    small = jnp.zeros((8, D + 128), F32)
+    gains = jnp.stack([gain_one, gain_two]).astype(F32)
+    small = lax.dynamic_update_slice(small, gains, (0, f * share))
+    small = lax.dynamic_update_slice(small, bias_table.astype(F32).T, (0, D + f * buckets_here))
+    chunks, chunk_rows = grad_chunks(share, hidden)
+    wide = max(384, share)
+    n_sems = 320
+    sems = Sems()
+    vmem, anywhere = pl.BlockSpec(memory_space=pltpu.VMEM), pl.BlockSpec(memory_space=pl.ANY)
+    out, grad_in, grads, sums = pl.pallas_call(
+        functools.partial(layer_kernel, nf, nc, micro, T, share, hidden, n_sems, sems),
+        out_shape=[
+            jax.ShapeDtypeStruct((micro, T, D), BF16),
+            jax.ShapeDtypeStruct((micro, T, D), BF16),
+            jax.ShapeDtypeStruct((chunk_rows, wide), BF16),
+            jax.ShapeDtypeStruct((8, D + 128), F32),
+        ],
+        in_specs=[vmem, vmem, anywhere, vmem, anywhere, anywhere, anywhere, vmem],
+        out_specs=[vmem, vmem, anywhere, vmem],
+        scratch_shapes=kernel_scratch(nf, nc, micro, T, share, hidden, n_sems),
+        compiler_params=pltpu.CompilerParams(
+            collective_id=0, has_side_effects=True, vmem_limit_bytes=61800 * 1024
+        ),
+    )(tokens[:, 0], pos, cotangent[:, 0], wqkv, w_out, w_in, w_back, small)
+    named = {name: grads[row : row + rows, :cols].astype(F32) for name, row, rows, cols in chunks}
+    scale = gain_one.astype(F32)[:, None]
+    grad_kv = named["kv"] * scale
+    grad_q = named["q"][:, :192] * scale
+    gain_rows = lax.dynamic_slice(sums, (0, f * share), (2, share))
+    grad_table = lax.dynamic_slice(sums, (0, D + f * buckets_here), (HEADS_HERE, buckets_here)).T
+    return (
+        out[:, None],
+        grad_in[:, None],
+        gain_rows[0],
+        gain_rows[1],
+        grad_q,
+        grad_kv[:, :192],
+        jnp.concatenate([grad_kv[:, 256:384], grad_kv[:, 192:256]], axis=1),
+        named["out"],
+        jnp.concatenate([named["in0"], named["in1"]], axis=1),
+        jnp.concatenate([named["back0"], named["back1"]], axis=0),
+        grad_table,
+    )
+
+
 def solution(mesh):
+    nf, nc = mesh.shape["fsdp"], mesh.shape["ctx"]
+    fits = D // nf % BLK == 0 and nc <= 4 and nc % 2 == 0 and mesh.shape["tp"] == 4
     return jax.shard_map(
-        per_device,
+        functools.partial(per_device, nf, nc) if fits else per_device_plain,
         mesh=mesh,
         in_specs=(
             P(None, "fsdp", ("ctx", "tp"), None),

time: 1120 us -> 259 us (0.23); the launches traced: 1100 us -> 259 us
  blocking collectives: 301 us -> 0 us
  other arithmetic: 277 us -> 7.34 us
  waiting for transfers between devices: 269 us -> 0 us
  Pallas kernels: 0 us -> 237 us
  matrix products: 157 us -> 0 us
  local copies, waits for them, and re-layouts: 77.1 us -> 14.2 us
  between operations: 17.7 us -> 0.78 us
    all_gather x28 -> x0, blocking collectives: 241 us -> none  [the longest x12 82.3 us: spread_rows(): return lax.all_gather(local_rows, 'tp', axis=0, tiled=True)]
    pallas_call x0 -> x1, Pallas kernels: none -> 237 us  [per_device(): pl.pallas_call(functools.partial(layer_kernel, nf, nc, micro, T, share, h...]
    reduce_sum x55 -> x0, other arithmetic: 191 us -> none  [the longest x24 134 us: table_bias(): jnp.sum(jnp.where(matches, bias_rows.T[:, None, None, :], 0.0), axis=-1)]
    dot_general x138 -> x0, matrix products: 157 us -> none  [the longest x18 27 us: left_product(): jnp.einsum('ra,rb->ab', left, right, preferred_element_type=jnp.float32)]
    reduce_scatter x18 -> x0, waiting for transfers between devices: 137 us -> none  [the longest x12 115 us: collect_rows(): lax.psum_scatter(partial_rows.astype(jnp.bfloat16), 'tp', scatter_dimensi...]
    psum x1 -> x0, waiting for transfers between devices: 131 us -> none  [per_device(): lax.psum((grad_wq, grad_wk, grad_wv, grad_wo, grad_wi, grad_wb, grad_tabl...]
    psum x2 -> x0, blocking collectives: 60.7 us -> none  [the longest x1 41.7 us: per_device(): lax.psum((grad_gain_one, grad_gain_two), ('fsdp', 'ctx', 'tp'))]
    eq x36 -> x0, other arithmetic: 42.7 us -> none  [the longest x24 28.1 us: table_bias(): matches = bucket[None, :, :, None] == slot_ids[None, None, None, :]]
  transfers between devices with their start and end apart: 21 -> 0, of which waited for: 9 -> 0; matrix products, arithmetic and copies ran while one was open for 39% -> 0% of each run, Pallas kernels for 0% -> 0%
where the time goes in v1:
time: 259 us
  Pallas kernels  237 us (92%)
  local copies, waits for them, and re-layouts  14.2 us (5%)
  other arithmetic  7.34 us (3%)
    pallas_call x1, Pallas kernels, per_device(): pl.pallas_call(functools.partial(layer_kernel, nf, nc, micro, T, share, h...  237 us
    unnamed x19, local copies, waits for them, and re-layouts  5.48 us

profile of v1, /device:TPU:0, one launch (start us, length us, event | category | flops | bytes accessed | tf_op | source)
XLA Modules:
  0.0 258.9 jit_solution(12323506764888303822)
XLA Ops:
  0.7 0.7 stack.10
  1.4 0.7 stack.9
  2.1 0.7 convert_element_type.9
  2.7 0.7 convert_bitcast_fusion
  3.4 1.3 pad.4.pos_in
  4.7 0.3 dynamic_update_slice.7.small_loc
  5.1 0.8 slice.44
  6.0 0.9 slice.45
  7.1 1.0 copy.25
  8.1 0.1 copy.26
  8.3 1.0 concatenate.18.wqkv_loc
  9.3 236.6 %shard_map.203 = (bf16[3,64,768]{2,1,0:T(8,128)(2,1)}, bf16[3,64,768]{2,1,0:T(8,128)(2,1)}, bf16[2496,384]{1,0:T(8,128)(2,1)}, f32[8,896]{1,0:T(8,128)}) custom-call(bf16[3,64,768]{2,1,0:T(8,128)(2,1)} %bitcast.13, s32[3,8,128]{2,1,0:T(8,128)} %pad.4.pos_in, bf16[3,64,768]{2,1,0:T(8,128)(2,1)} %bitcast.14, bf16[384,640]{1,0:T(8,128)(2,1)} %concatenate.18.wqkv_loc, ...), custom_call_target="tpu_custom_call" | custom-call | tf_op jit(solution)/shard_map/pallas_call | solution.py:1268
  245.9 1.3 dynamic-slice_bitcast_fusion
  247.2 1.4 dynamic-slice_reduce_fusion
  248.7 1.6 slice_convert_fusion.1
  250.3 1.0 convert_multiply_fusion.1
  251.3 0.9 copy.29
  252.2 1.1 convert_multiply_fusion
  253.5 0.9 copy.30
  254.4 0.9 copy.31
  255.3 1.1 slice_convert_fusion
  256.4 1.1 maximum_convert_fusion
  257.5 0.7 copy.38
  258.2 0.7 copy.39
  (20 shorter events, 0.5 us)
Async XLA Ops:
  0.6 7.5 %copy-start.3 = (bf16[384,192]{0,1:T(8,128)(2,1)S(1)}, bf16[384,192]{0,1:T(8,128)(2,1)}, u32[]{:S(2)}) copy-start(bf16[384,192]{0,1:T(8,128)(2,1)} %param.15) | copy-start | bytes 442372
  5.1 4.2 %copy-start.4 = (f32[8,896]{1,0:T(8,128)}, f32[8,896]{1,0:T(8,128)S(1)}, u32[]{:S(2)}) copy-start(f32[8,896]{1,0:T(8,128)S(1)} %dynamic_update_slice.7.small_loc) | copy-start | bytes 86020
  253.5 1.8 copy-start
  256.4 1.1 copy-start.2
  256.4 1.8 copy-start.1
